TPU v7x, 128 devices: a whole 4x4x4 slice. The times are simulated.
128 devices in a mesh: group: 2 (over x_hi), expert: 64 (over x_lo, y, z, core).
Axes of the slice: x: 4 (x_hi: 2, x_lo: 2; x = x_hi * 2 + x_lo), y: 4, z: 4, core: 2. Of those that a mesh axis runs over, the one named last changes fastest.
Arguments:
- tokens: bfloat16 [2, 8192, 4096], P('group', 'expert'), may hold values from -6 to 6
- expert_ids: int32 [2, 8192, 1], P('group', 'expert'), may hold values from 0 to 7; in each aligned block of 128 rows (0 to 127, 128 to 255, ..., all dimensions but the last counted through in order) at most 32 rows name the same one
- route_weight: float32 [2, 8192, 1], P('group', 'expert'), may hold values from 0.1 to 1
- inner_weights: bfloat16 [2, 3, 12288, 4096], P('group', None, 'expert'), may hold values from -0.09375 to 0.09375
- outer_weights: float32 [3, 12288, 4096], P(None, 'expert', 'group'), may hold values from -0.09375 to 0.09375
- momentum: float32 [3, 12288, 4096], P(None, 'expert', 'group'), may hold values from -0.09375 to 0.09375
Outputs:
- expert_out: bfloat16 [2, 8192, 4096], P('group', 'expert')
- new_outer: float32 [3, 12288, 4096], P(None, 'expert', 'group')
- new_momentum: float32 [3, 12288, 4096], P(None, 'expert', 'group')
Inputs may be any that keep to these rules, and one draw needn't show every extreme that they name: `expert_ids`: among the tokens of one device, no expert is named more than 32 times, and in every draw some device has an expert named exactly 32 times.
All inputs are finite; a program needn't handle non-finite values.
Results may differ from a plain program's by a relative error of at most 0.025.
Values may be sent and summed in bfloat16 or wider, within the bound.
A program may use at most 192 MiB of HBM per device.

v0:
```python
import jax
import jax.numpy as jnp
from jax import lax
from jax.sharding import PartitionSpec as P

SPLIT = 8
PICKS = 1


outer_rate = 0.7
momentum_rate = 0.9


def expert_rows(rows_in, weights):
    dims = (((1,), (1,)), ((), ()))
    gate = lax.dot_general(rows_in, weights[0], dims, preferred_element_type=jnp.float32)
    upward = lax.dot_general(rows_in, weights[1], dims, preferred_element_type=jnp.float32)
    hidden = (jax.nn.silu(gate) * upward).astype(jnp.bfloat16)
    return jnp.dot(hidden, weights[2], preferred_element_type=jnp.float32).astype(jnp.bfloat16)


def per_device(tokens, expert_ids, route_weight, inner_weights, outer_weights, momentum):
    width = tokens.shape[2]
    tok_rows = tokens.shape[1]
    groups = lax.axis_size("group")
    devices_inner = lax.axis_size("expert")
    experts_in = devices_inner // SPLIT
    capacity = min(tok_rows, 2 * tok_rows * PICKS // experts_in)
    summed = lax.psum_scatter(inner_weights[0], "group", scatter_dimension=2, tiled=True).astype(
        jnp.float32
    )
    pseudo = outer_weights - summed / groups
    new_momentum = momentum_rate * momentum + pseudo
    new_outer = outer_weights - outer_rate * (pseudo + momentum_rate * new_momentum)
    fresh_half = new_outer.astype(jnp.bfloat16)
    token_expert = expert_ids[0, :, 0]
    one_hot = (token_expert[:, None] == jnp.arange(experts_in, dtype=jnp.int32)[None, :]).astype(
        jnp.int32
    )
    rank_all = jnp.cumsum(one_hot, axis=0) - one_hot
    rank_in = jnp.sum(rank_all * one_hot, axis=1)
    slot_index = token_expert * capacity + rank_in
    placing = (
        slot_index[None, :] == jnp.arange(experts_in * capacity, dtype=jnp.int32)[:, None]
    ).astype(jnp.bfloat16)
    packed = jnp.dot(placing, tokens[0], preferred_element_type=jnp.float32).astype(jnp.bfloat16)
    send_rows = jnp.broadcast_to(
        packed.reshape(experts_in, 1, capacity, width), (experts_in, SPLIT, capacity, width)
    )
    send_rows = send_rows.reshape(devices_inner, capacity, width)
    whole = lax.all_gather(fresh_half, "group", axis=2, tiled=True)
    received = lax.all_to_all(send_rows, "expert", split_axis=0, concat_axis=0, tiled=True)
    partial_value = expert_rows(received.reshape(devices_inner * capacity, width), whole)
    returned = lax.all_to_all(
        partial_value.reshape(devices_inner, capacity, width),
        "expert",
        split_axis=0,
        concat_axis=0,
        tiled=True,
    )
    combined = jnp.sum(
        returned.reshape(experts_in, SPLIT, capacity, width).astype(jnp.float32), axis=1
    )
    combined = combined.reshape(experts_in * capacity, width)
    picked = jnp.take(combined, slot_index, axis=0)
    expert_out = (route_weight[0, :, 0][:, None] * picked).astype(jnp.bfloat16)
    return (expert_out[None], new_outer, new_momentum)


def solution(mesh):
    in_specs = (
        P("group", "expert", None),
        P("group", "expert", None),
        P("group", "expert", None),
        P("group", None, "expert", None),
        P(None, "expert", "group"),
        P(None, "expert", "group"),
    )
    out_specs = (P("group", "expert", None), P(None, "expert", "group"), P(None, "expert", "group"))
    return jax.shard_map(
        per_device, mesh=mesh, in_specs=in_specs, out_specs=out_specs, check_vma=False
    )
```

profile of v0, /device:TPU:67, one launch (start us, length us, event | category | flops | bytes accessed | tf_op | source)
XLA Modules:
  0.0 651.5 jit_solution(15222899562332438833)
XLA Ops:
  7.2 0.0 copy-start
  7.2 0.8 fusion.12
  8.0 0.2 reduce_window_sum.11
  8.2 0.8 select_reduce_fusion
  9.0 0.7 compare_and_fusion
  9.7 0.0 copy-done
  9.7 0.7 convolution_convert_fusion.1
  10.4 6.0 broadcast_in_dim.23
  16.4 9.7 %all-to-all-start = ((bf16[64,32,4096]{2,1,0:T(8,128)(2,1)}), bf16[64,32,4096]{2,1,0:T(8,128)(2,1)}, u32[]{:S(2)}, u32[]{:S(2)}) async-start(bf16[64,32,4096]{2,1,0:T(8,128)(2,1)} %bitcast.43), calls=%async_computation | async-start | bytes 33554432 | tf_op jit(solution)/shard_map/all_to_all | solution.py:52
  26.1 0.0 reduce-scatter.2.cloned.1.call-start
  26.1 0.7 reduce-scatter.2.cloned.1.call-update
  26.8 0.0 all-gather.2.cloned.1.call-start
  26.9 117.3 %reduce-scatter.2.cloned.1.call-done = bf16[3,192,2048]{2,1,0:T(8,128)(2,1)} async-done(((bf16[3,192,4096]{2,1,0:T(8,128)(2,1)}), bf16[3,192,2048]{2,1,0:T(8,128)(2,1)}) %reduce-scatter.2.cloned.1.call-update) | async-done | bytes 2359312 | tf_op jit(solution)/shard_map/reduce_scatter | solution.py:29
  144.2 8.2 %fusion.15 = (bf16[3,192,2048]{2,1,0:T(8,128)(2,1)}, f32[3,192,2048]{2,1,0:T(8,128)}, f32[3,192,2048]{2,1,0:T(8,128)}) fusion(f32[3,192,2048]{2,1,0:T(8,128)} %param.10, bf16[3,192,2048]{2,1,0:T(8,128)(2,1)} %reduce-scatter.2.cloned.1.call-done, f32[3,192,2048]{2,1,0:T(8,128)} %param.11), kind=kLoop, calls=%fused_computation.36 | loop fusion | flops 11796480 | bytes 23592960 | tf_op jit(solution)/shard_map/convert_element_type | solution.py:35
  152.4 0.0 all-gather.2.cloned.1.call-update
  152.4 122.9 %all-gather.2.cloned.1.call-done = bf16[3,192,4096]{2,1,0:T(8,128)(2,1)} async-done(((bf16[3,192,2048]{2,1,0:T(8,128)(2,1)}), bf16[3,192,4096]{2,1,0:T(8,128)(2,1)}) %all-gather.2.cloned.1.call-update) | async-done | bytes 4718608 | tf_op jit(solution)/shard_map/all_gather | solution.py:51
  275.3 40.0 %all-to-all-done = bf16[64,32,4096]{2,1,0:T(8,128)(2,1)} async-done(((bf16[64,32,4096]{2,1,0:T(8,128)(2,1)}), bf16[64,32,4096]{2,1,0:T(8,128)(2,1)}, u32[]{:S(2)}, u32[]{:S(2)}) %all-to-all-start) | async-done | bytes 16777248 | tf_op jit(solution)/shard_map/all_to_all | solution.py:52
  315.3 9.6 %fusion.3 = f32[2048,192]{0,1:T(8,128)S(1)} fusion(bf16[2048,4096]{1,0:T(8,128)(2,1)} %bitcast.5, bf16[3,192,4096]{2,1,0:T(8,128)(2,1)} %all-gather.2.cloned.1.call-done), kind=kOutput, calls=%fused_computation.15 | convolution fusion | flops 3221225472 | bytes 19922944 | tf_op jit(solution)/shard_map/dot_general | solution.py:16
  324.9 17.9 %convolution_convert_fusion = bf16[2048,4096]{1,0:T(8,128)(2,1)} fusion(bf16[2048,4096]{1,0:T(8,128)(2,1)} %bitcast.5, bf16[3,192,4096]{2,1,0:T(8,128)(2,1)} %all-gather.2.cloned.1.call-done, f32[2048,192]{0,1:T(8,128)S(1)} %fusion.3), kind=kOutput, calls=%fused_computation.2 | convolution fusion | flops 6453198848 | bytes 38273024 | tf_op jit(solution)/shard_map/dot_general | solution.py:19
  342.8 0.0 copy-start.2
  342.8 22.9 %all-to-all-start.1 = ((bf16[64,32,4096]{2,1,0:T(8,128)(2,1)}), bf16[64,32,4096]{2,1,0:T(8,128)(2,1)}, u32[]{:S(2)}, u32[]{:S(2)}) async-start(bf16[64,32,4096]{2,1,0:T(8,128)(2,1)} %bitcast.44), calls=%async_computation.2 | async-start | bytes 33554432 | tf_op jit(solution)/shard_map/all_to_all | solution.py:54
  365.7 0.0 copy-done.2
  365.7 262.3 %all-to-all-done.1 = bf16[64,32,4096]{2,1,0:T(8,128)(2,1)} async-done(((bf16[64,32,4096]{2,1,0:T(8,128)(2,1)}), bf16[64,32,4096]{2,1,0:T(8,128)(2,1)}, u32[]{:S(2)}, u32[]{:S(2)}) %all-to-all-start.1) | async-done | bytes 16777248 | tf_op jit(solution)/shard_map/all_to_all | solution.py:54
  628.0 10.9 %convert_reduce_fusion = f32[8,32,4096]{2,1,0:T(8,128)} fusion(bf16[64,32,4096]{2,1,0:T(8,128)(2,1)} %all-to-all-done.1), kind=kLoop, calls=%fused_computation.1 | loop fusion | flops 15728640 | bytes 20971520 | tf_op jit(solution)/shard_map/reduce_sum | solution.py:61
  638.9 0.0 copy-start.3
  638.9 0.0 copy-start.1
  638.9 4.5 gather_fusion
  643.4 0.0 copy-done.3
  643.4 1.3 fusion.2
  644.7 0.0 copy-done.1
  (2 shorter events, 0.0 us)
Async XLA Ops:
  7.2 2.5 copy-start
  16.4 298.9 %all-to-all-start = ((bf16[64,32,4096]{2,1,0:T(8,128)(2,1)}), bf16[64,32,4096]{2,1,0:T(8,128)(2,1)}, u32[]{:S(2)}, u32[]{:S(2)}) async-start(bf16[64,32,4096]{2,1,0:T(8,128)(2,1)} %bitcast.43), calls=%async_computation | async-start | bytes 33554432 | tf_op jit(solution)/shard_map/all_to_all | solution.py:52
  26.1 118.1 %reduce-scatter.2.cloned.1.call-start = ((), (), s32[]{:S(2)}) async-start(), calls=%async_computation.3 | async-start | bytes 7077888 | tf_op jit(solution)/shard_map/reduce_scatter | solution.py:29
  26.8 248.4 %all-gather.2.cloned.1.call-start = ((), (), s32[]{:S(2)}) async-start(), calls=%async_computation.4 | async-start | bytes 7077888 | tf_op jit(solution)/shard_map/all_gather | solution.py:51
  342.8 22.9 %copy-start.2 = (s32[1,128,1]{1,2,0:T(1,128)S(1)}, s32[1,128,1]{1,2,0:T(1,128)}, u32[]{:S(2)}) copy-start(s32[1,128,1]{1,2,0:T(1,128)} %param.7) | copy-start | bytes 1540
  342.8 285.3 %all-to-all-start.1 = ((bf16[64,32,4096]{2,1,0:T(8,128)(2,1)}), bf16[64,32,4096]{2,1,0:T(8,128)(2,1)}, u32[]{:S(2)}, u32[]{:S(2)}) async-start(bf16[64,32,4096]{2,1,0:T(8,128)(2,1)} %bitcast.44), calls=%async_computation.2 | async-start | bytes 33554432 | tf_op jit(solution)/shard_map/all_to_all | solution.py:54
  638.9 4.5 copy-start.3
  638.9 5.8 copy-start.1
Sparse Core Ops, SparseCore 0:
  29.3 114.7 reduce-scatter.1
  152.5 122.6 all-gather.1
where the time goes:
time: 652 us
  waiting for transfers between devices  543 us (83%)
  starting transfers between devices  32.7 us (5%)
  matrix products  28.2 us (4%)
  other arithmetic  22.8 us (3%)
  between operations  14.1 us (2%)
  local copies, waits for them, and re-layouts  10.5 us (2%)
    all_to_all x1, waiting for transfers between devices, per_device(): lax.all_to_all(partial_value.reshape(devices_inner, capacity, width), 'ex...  262 us
    all_gather x1, waiting for transfers between devices, per_device(): whole = lax.all_gather(fresh_half, 'group', axis=2, tiled=True)  123 us
    reduce_scatter x1, waiting for transfers between devices, per_device(): lax.psum_scatter(inner_weights[0], 'group', scatter_dimension=2, tiled=True)  117 us
    all_to_all x1, waiting for transfers between devices, per_device(): lax.all_to_all(send_rows, 'expert', split_axis=0, concat_axis=0, tiled=True)  40 us
    all_to_all x1, starting transfers between devices, per_device(): lax.all_to_all(partial_value.reshape(devices_inner, capacity, width), 'ex...  22.9 us
    dot_general x1, matrix products, expert_rows(): jnp.dot(hidden, weights[2], preferred_element_type=jnp.float32)  17.9 us
  transfers between devices with their start and end apart: 4, of which 4 were waited for; matrix products, arithmetic and copies ran while one was open for 1% of the time, Pallas kernels for 0%

commit v1 on v0

v1 whole, which is shorter than its diff:
```python
import functools

import jax
import jax.numpy as jnp
from jax import lax
from jax.experimental import pallas as pl
from jax.experimental.pallas import tpu as pltpu
from jax.sharding import PartitionSpec as P

MESH = pl.DeviceIdType.MESH
F32 = jnp.float32
BF16 = jnp.bfloat16

outer_rate = 0.7
momentum_rate = 0.9

WIDTH = 4096
HALF = 2048
CAP = 32
PARTS = 4
PART = HALF // PARTS
BLOCK = 256
ORDER = (("g", 0), ("g", 1), ("d", 0), ("d", 1), ("g", 2), ("d", 2), ("d", 3))
STEPS = len(ORDER)
AHEAD = 2


def kernel(
    tok, ids, rw, inner, outer, mom, eo, no, nm,
    tokv, packed, xs, wg, wd, rg, rd, og, od, ob, mb, hs, hid, ys, ret, eov, place,
    s_rs, r_rs, s_ag, r_ag, l_in, l_out, s_sg, r_sg, s_dz, r_dz, s_df, r_df, s_sd, r_sd,
    s_dp, r_dp, s_xz, r_xz, s_xf, r_xf, s_h, r_h, s_rt, r_rt, l_rt, l_eo, l_tok,
):
    g = lax.axis_index("group")
    e = lax.axis_index("expert")
    low = lax.div(e, 32)
    y = lax.rem(lax.div(e, 8), 4)
    z = lax.rem(lax.div(e, 2), 4)
    c = lax.rem(e, 2)
    x = g * 2 + low

    def device(xx, yy, zz, cc):
        return (lax.div(xx, 2), ((lax.rem(xx, 2) * 4 + yy) * 4 + zz) * 2 + cc)

    def turn(a, n):
        return lax.rem(a + n, 4)

    partner = device(turn(x, 2), y, z, c)
    sibling = device(x, y, z, 1 - c)
    up, down, far = (device(x, y, turn(z, n), c) for n in (1, 3, 2))
    xn = (x, turn(x, 1), turn(x, 3))

    barrier = pltpu.get_barrier_semaphore()
    near = [partner, sibling, up, down, far]
    near += [device(x, turn(y, dy), z, c) for dy in (1, 2, 3)]
    near += [device(xn[s], turn(y, dy), z, c) for s in (1, 2) for dy in range(4)]
    for other in near:
        pl.semaphore_signal(barrier, inc=1, device_id=other, device_id_type=MESH)

    sends = []
    locals_ = []

    def send(src, dst, ss, rs, dev):
        copy = pltpu.make_async_remote_copy(
            src_ref=src, dst_ref=dst, send_sem=ss, recv_sem=rs, device_id=dev, device_id_type=MESH
        )
        copy.start()
        sends.append(copy)

    def arrived(dst, ss, rs):
        pltpu.make_async_remote_copy(
            src_ref=dst, dst_ref=dst, send_sem=ss, recv_sem=rs, device_id=sibling, device_id_type=MESH
        ).wait_recv()

    def local(src, dst, sem):
        copy = pltpu.make_async_copy(src, dst, sem)
        copy.start()
        return copy

    mine = pl.multiple_of(g * HALF, HALF)
    theirs = pl.multiple_of((1 - g) * HALF, HALF)
    half_of = (mine, theirs)

    def in_view(ref, step, offset):
        kind, n = ORDER[step]
        if kind == "g":
            return ref.at[0:2, n, :, pl.ds(offset, HALF)]
        return ref.at[2, :, :, pl.ds(offset + n * PART, PART)]

    def half_view(ref_g, ref_d, step):
        kind, n = ORDER[step]
        if kind == "g":
            return ref_g.at[n]
        return ref_d.at[:, :, pl.ds(n * PART, PART)]

    def wg_view(n, kind, core):
        return wg.at[n, :, core, :, pl.ds(half_of[kind], HALF)]

    def wd_view(n, kind, zz, core):
        return wd.at[zz, :, core, :, pl.ds(half_of[kind] + n * PART, PART)]

    def fresh_view(step, kind):
        name, n = ORDER[step]
        return wg_view(n, kind, c) if name == "g" else wd_view(n, kind, z, c)

    tok_copy = local(tok, tokv, l_tok)
    loads = []
    for step in range(STEPS):
        loads.append(
            (
                local(in_view(inner, step, mine), half_view(og, od, step), l_in.at[step, 0]),
                local(in_view(outer, step, 0), in_view(ob, step, 0), l_in.at[step, 1]),
                local(in_view(mom, step, 0), in_view(mb, step, 0), l_in.at[step, 2]),
            )
        )

    lane = lax.broadcasted_iota(jnp.int32, (128, 128), 1)
    row = lax.broadcasted_iota(jnp.int32, (128, 128), 0)
    named = ids[...]
    one_hot = (lane == named).astype(F32)
    earlier = (lane < row).astype(F32)
    rank = jnp.dot(earlier.astype(BF16), one_hot.astype(BF16), preferred_element_type=F32)
    rank = jnp.sum(rank * one_hot, axis=1, keepdims=True)
    slot = named.astype(F32) * CAP + rank
    wide = lax.broadcasted_iota(jnp.int32, (128, BLOCK), 1).astype(F32)
    placing = (wide == slot).astype(F32)
    place[...] = placing.astype(BF16)
    pack = jnp.transpose(placing).astype(BF16)
    tok_copy.wait()

    @pl.loop(0, WIDTH // 512)
    def _(n):
        cols = pl.ds(pl.multiple_of(n * 512, 512), 512)
        packed[:, cols] = jnp.dot(pack, tokv[:, cols], preferred_element_type=F32).astype(BF16)

    pl.semaphore_wait(barrier, len(near))

    def start_rs(step):
        if step < STEPS:
            send(
                in_view(inner, step, theirs), half_view(rg, rd, step),
                s_rs.at[step], r_rs.at[step], partner,
            )

    for step in range(AHEAD):
        start_rs(step)

    def rows_at(start, size):
        return pl.ds(pl.multiple_of(start, 16), size)

    def spread(n):
        if n < 3:
            return 0, n + 1, 0, 32
        if n < 7:
            return 1, n - 3, 0, 16
        return 2, n - 7, 16, 16

    def expert_rows(s, yy, first, size):
        owner = low if s == 0 else 1 - low
        return rows_at((owner * 4 + yy) * CAP + first, size)

    def buffer_rows(s, yy, first, size):
        return rows_at((0 if s == 0 else 128) + yy * 32 + first, size)

    xs[z, rows_at(y * 32, 32), :] = packed[expert_rows(0, y, 0, 32), :]
    for n in (0, 3, 7, 2, 4, 8, 6, 10, 1, 5, 9):
        s, dy, first, size = spread(n)
        send(
            packed.at[expert_rows(s, turn(y, dy), first, size)],
            xs.at[z, buffer_rows(s, y, first, size)],
            s_dp.at[n], r_dp.at[n], device(xn[s], turn(y, dy), z, c),
        )

    def x_piece(zz, p):
        s, dy = p // 4, p % 4
        return xs.at[zz, buffer_rows(s, turn(y, 4 - dy), 0, 32)]

    def dispatch(p):
        s, dy = p // 4, p % 4
        for n in ((dy - 1,) if s == 0 else (3 + dy, 7 + dy)):
            if n >= 0:
                sn, _, first, size = spread(n)
                arrived(
                    xs.at[z, buffer_rows(sn, turn(y, 4 - dy), first, size)], s_dp.at[n], r_dp.at[n]
                )
        view = x_piece(z, p)
        send(view, view, s_xz.at[p, 0], r_xz.at[p, 0], up)
        send(view, view, s_xz.at[p, 1], r_xz.at[p, 1], down)

    def x_forward(p):
        way = p // 4
        view = x_piece(turn(z, 1 if way else 3), p)
        arrived(view, s_xz.at[p, way], r_xz.at[p, way])
        send(view, view, s_xf.at[p], r_xf.at[p], down if way else up)

    def x_rest():
        for p in range(8):
            way = 1 - p // 4
            arrived(x_piece(turn(z, 1 if way else 3), p), s_xz.at[p, way], r_xz.at[p, way])
        for p in range(8):
            arrived(x_piece(turn(z, 2), p), s_xf.at[p], r_xf.at[p])

    def outer_step(o, m, a, b):
        pseudo = o - (a.astype(F32) + b.astype(F32)) / 2
        new_m = momentum_rate * m + pseudo
        return o - outer_rate * (pseudo + momentum_rate * new_m), new_m

    def share(step, kind):
        name, n = ORDER[step]
        view = fresh_view(step, kind)
        if name == "g":
            send(view, view, s_sg.at[n, kind], r_sg.at[n, kind], sibling)
        else:
            send(view, view, s_dz.at[n, kind, 0], r_dz.at[n, kind, 0], up)
            send(view, view, s_dz.at[n, kind, 1], r_dz.at[n, kind, 1], down)
            send(view, view, s_sd.at[n, kind, 0], r_sd.at[n, kind, 0], sibling)

    def update(step):
        name, n = ORDER[step]
        for copy in loads[step]:
            copy.wait()
        arrived(half_view(rg, rd, step), s_rs.at[step], r_rs.at[step])
        for i in range(2 if name == "g" else 3):

            @pl.loop(0, 4)
            def _(t):
                rows = pl.ds(pl.multiple_of(t * 16, 16), 16)
                if name == "g":
                    at = (i, n, rows, slice(None))
                    a, b = og[n, i, rows, :], rg[n, i, rows, :]
                else:
                    at = (2, i, rows, pl.ds(n * PART, PART))
                    a, b = od[i, rows, pl.ds(n * PART, PART)], rd[i, rows, pl.ds(n * PART, PART)]
                new_o, new_m = outer_step(ob[at], mb[at], a, b)
                ob[at] = new_o
                mb[at] = new_m
                if name == "g":
                    wg[n, i, c, rows, pl.ds(mine, HALF)] = new_o.astype(BF16)
                else:
                    wd[z, i, c, rows, pl.ds(mine + n * PART, PART)] = new_o.astype(BF16)

        view = fresh_view(step, 0)
        send(view, view, s_ag.at[step], r_ag.at[step], partner)
        start_rs(step + AHEAD)
        share(step, 0)
        locals_.append(local(in_view(ob, step, 0), in_view(no, step, 0), l_out.at[step, 0]))
        locals_.append(local(in_view(mb, step, 0), in_view(nm, step, 0), l_out.at[step, 1]))

    def gathered(step):
        arrived(fresh_view(step, 1), s_ag.at[step], r_ag.at[step])
        share(step, 1)

    def d_near(n, kind):
        for way in (0, 1):
            view = wd_view(n, kind, turn(z, 1 if way else 3), c)
            arrived(view, s_dz.at[n, kind, way], r_dz.at[n, kind, way])
            if way == kind:
                send(view, view, s_df.at[n, kind], r_df.at[n, kind], down if way else up)
            send(view, view, s_sd.at[n, kind, 1 + way], r_sd.at[n, kind, 1 + way], sibling)

    def d_far(n, kind):
        view = wd_view(n, kind, turn(z, 2), c)
        arrived(view, s_df.at[n, kind], r_df.at[n, kind])
        send(view, view, s_sd.at[n, kind, 3], r_sd.at[n, kind, 3], sibling)

    def hid_cols(zz, n):
        return pl.ds(pl.multiple_of((zz * 3 + n) * 128, 128), 128)

    def hidden(n):
        for kind in (0, 1):
            arrived(wg_view(n, kind, 1 - c), s_sg.at[n, kind], r_sg.at[n, kind])

        @pl.loop(0, 4)
        def _(r):
            zz = turn(z, r + 1)
            both = lax.dot_general(
                xs[zz], wg[n].reshape(256, WIDTH), (((1,), (1,)), ((), ())),
                preferred_element_type=F32,
            )
            gate = both[:, :128]
            value = (gate / (1.0 + jnp.exp(-gate)) * both[:, 128:]).astype(BF16)
            hs[n, r] = value

            @pl.when(r < 3)
            def _():
                pltpu.make_async_remote_copy(
                    src_ref=hs.at[n, r], dst_ref=hid.at[:, hid_cols(z, n)],
                    send_sem=s_h.at[n, r], recv_sem=r_h.at[n, r],
                    device_id=device(x, y, zz, c), device_id_type=MESH,
                ).start()

        hid[:, hid_cols(z, n)] = hs[n, 3]
        for r in range(3):
            sends.append(
                pltpu.make_async_remote_copy(
                    src_ref=hs.at[n, r], dst_ref=hid.at[:, hid_cols(z, n)],
                    send_sem=s_h.at[n, r], recv_sem=r_h.at[n, r],
                    device_id=device(x, y, turn(z, r + 1), c), device_id_type=MESH,
                )
            )

    def hidden_rest():
        for n in range(3):
            for r in range(3):
                arrived(hid.at[:, hid_cols(turn(z, 3 - r), n)], s_h.at[n, r], r_h.at[n, r])

    def project(n):
        for kind in (0, 1):
            for k, dz in enumerate((0, 3, 1, 2)):
                arrived(
                    wd_view(n, kind, turn(z, dz), 1 - c), s_sd.at[n, kind, k], r_sd.at[n, kind, k]
                )
        for h in (0, 1):

            @pl.loop(0, PART // 256)
            def _(t):
                cols = pl.ds(pl.multiple_of(n * PART + t * 256, 256), 256)
                wide_cols = pl.ds(pl.multiple_of(h * HALF + n * PART + t * 256, 256), 256)
                ys[h, :, cols] = jnp.dot(
                    hid[...], wd[:, :, :, :, wide_cols].reshape(1536, 256),
                    preferred_element_type=F32,
                ).astype(BF16)

        cols = pl.ds(n * PART, PART)
        for m in range(11):
            s, dy, first, size = spread(m)
            back = xn[(0, 2, 1)[s]]
            send(
                ys.at[:, buffer_rows(s, turn(y, 4 - dy), first, size), cols],
                ret.at[:, rows_at((low * 4 + y) * CAP + first, size), cols],
                s_rt.at[n, m], r_rt.at[n, m], device(back, turn(y, 4 - dy), z, c),
            )
        ret[:, expert_rows(0, y, 0, 32), cols] = ys[:, buffer_rows(0, y, 0, 32), cols]

    def finish(n):
        cols = pl.ds(n * PART, PART)
        for m in range(11):
            s, dy, first, size = spread(m)
            arrived(
                ret.at[:, expert_rows(s, turn(y, dy), first, size), cols],
                s_rt.at[n, m], r_rt.at[n, m],
            )
        for h in (0, 1):
            picked = jnp.dot(place[...], ret[h, :, cols], preferred_element_type=F32)
            wide_cols = pl.ds(h * HALF + n * PART, PART)
            eov[:, wide_cols] = (rw[...] * picked).astype(BF16)
            locals_.append(local(eov.at[:, wide_cols], eo.at[:, wide_cols], l_eo.at[n, h]))

    dispatch(0)
    for p in (1, 4, 5, 3):
        dispatch(p)
    update(0)
    for p in (7, 2, 6):
        dispatch(p)
    x_forward(0)
    x_forward(1)
    x_forward(4)
    update(1)
    x_forward(5)
    x_forward(3)
    gathered(0)
    update(2)
    x_forward(7)
    x_forward(2)
    x_forward(6)
    gathered(1)
    update(3)
    gathered(2)
    x_rest()
    hidden(0)
    update(4)
    gathered(3)
    hidden(1)
    update(5)
    d_near(0, 0)
    d_near(0, 1)
    gathered(4)
    d_far(0, 0)
    d_far(0, 1)
    d_near(1, 0)
    d_near(1, 1)
    hidden(2)
    update(6)
    gathered(5)
    d_far(1, 0)
    d_far(1, 1)
    gathered(6)
    hidden_rest()
    project(0)
    d_near(2, 0)
    d_near(2, 1)
    project(1)
    d_far(2, 0)
    d_far(2, 1)
    d_near(3, 0)
    d_near(3, 1)
    project(2)
    finish(0)
    d_far(3, 0)
    d_far(3, 1)
    finish(1)
    project(3)
    finish(2)
    finish(3)

    for copy in sends:
        copy.wait_send()
    for copy in locals_:
        copy.wait()


def per_device(tokens, expert_ids, route_weight, inner_weights, outer_weights, momentum):
    dma = pltpu.SemaphoreType.DMA
    vmem = pltpu.VMEM
    any_space = pl.BlockSpec(memory_space=pl.ANY)
    in_vmem = pl.BlockSpec(memory_space=pltpu.VMEM)
    weights = (3, 3, 64, HALF)
    scratch = [
        vmem((128, WIDTH), BF16),
        vmem((BLOCK, WIDTH), BF16),
        vmem((4, BLOCK, WIDTH), BF16),
        vmem((3, 2, 2, 64, WIDTH), BF16),
        vmem((4, 3, 2, 64, WIDTH), BF16),
        vmem((3, 2, 64, HALF), BF16),
        vmem((3, 64, HALF), BF16),
        vmem((3, 2, 64, HALF), BF16),
        vmem((3, 64, HALF), BF16),
        vmem(weights, F32),
        vmem(weights, F32),
        vmem((3, 4, BLOCK, 128), BF16),
        vmem((BLOCK, 1536), BF16),
        vmem((2, BLOCK, HALF), BF16),
        vmem((2, BLOCK, HALF), BF16),
        vmem((128, WIDTH), BF16),
        vmem((128, BLOCK), BF16),
    ]
    scratch += [dma((STEPS,))] * 4
    scratch += [dma((STEPS, 3)), dma((STEPS, 2))]
    scratch += [dma((3, 2))] * 2
    scratch += [dma((PARTS, 2, 2))] * 2
    scratch += [dma((PARTS, 2))] * 2
    scratch += [dma((PARTS, 2, 4))] * 2
    scratch += [dma((11,))] * 2
    scratch += [dma((8, 2))] * 2
    scratch += [dma((8,))] * 2
    scratch += [dma((3, 3))] * 2
    scratch += [dma((PARTS, 11))] * 2
    scratch += [dma((1,)), dma((PARTS, 2)), dma]
    out, new_outer, new_momentum = pl.pallas_call(
        kernel,
        out_shape=(
            jax.ShapeDtypeStruct((128, WIDTH), BF16),
            jax.ShapeDtypeStruct(weights, F32),
            jax.ShapeDtypeStruct(weights, F32),
        ),
        in_specs=[any_space, in_vmem, in_vmem, any_space, any_space, any_space],
        out_specs=(any_space,) * 3,
        scratch_shapes=scratch,
        compiler_params=pltpu.CompilerParams(
            collective_id=0, has_side_effects=True, vmem_limit_bytes=62 << 20
        ),
    )(
        tokens.reshape(128, WIDTH),
        expert_ids.reshape(128, 1),
        route_weight.reshape(128, 1),
        inner_weights.reshape(3, 3, 64, WIDTH),
        outer_weights.reshape(weights),
        momentum.reshape(weights),
    )
    full = (3, 192, HALF)
    return out[None], new_outer.reshape(full), new_momentum.reshape(full)


def solution(mesh):
    in_specs = (
        P("group", "expert", None),
        P("group", "expert", None),
        P("group", "expert", None),
        P("group", None, "expert", None),
        P(None, "expert", "group"),
        P(None, "expert", "group"),
    )
    out_specs = (P("group", "expert", None), P(None, "expert", "group"), P(None, "expert", "group"))
    return jax.shard_map(
        per_device, mesh=mesh, in_specs=in_specs, out_specs=out_specs, check_vma=False
    )
```

time: 652 us -> 221 us (0.34)
  the two profiles are of different devices: /device:TPU:67 before, /device:TPU:1 now
where the time goes in v1:
time: 221 us
  Pallas kernels  208 us (94%)
  local copies, waits for them, and re-layouts  12.6 us (6%)
    pallas_call x1, Pallas kernels, per_device(): pl.pallas_call(kernel, out_shape=(jax.ShapeDtypeStruct((128, WIDTH), BF16...  208 us
    unnamed x7, local copies, waits for them, and re-layouts  9.78 us

profile of v1, /device:TPU:1, one launch (start us, length us, event | category | flops | bytes accessed | tf_op | source)
XLA Modules:
  0.0 220.9 jit_solution(15187793067017655201)
XLA Ops:
  0.6 1.4 copy.9.ids
  2.0 1.4 copy.10.rw
  3.4 207.7 %shard_map.85 = (bf16[128,4096]{1,0:T(8,128)(2,1)}, f32[3,3,64,2048]{3,2,1,0:T(8,128)}, f32[3,3,64,2048]{3,2,1,0:T(8,128)}) custom-call(bf16[128,4096]{1,0:T(8,128)(2,1)} %bitcast.17, s32[128,1]{1,0:T(8,128)} %copy.9.ids, f32[128,1]{1,0:T(8,128)} %copy.10.rw, bf16[3,3,64,4096]{3,2,1,0:T(8,128)(2,1)} %bitcast.13, f32[3,3,64,2048]{3,2,1,0:T(8,128)} %bitcast.14, ...), custom_call_target="tpu_custom_call" | custom-call | tf_op jit(solution)/shard_map/pallas_call | solution.py:449
  211.1 0.0 slice-start
  211.1 2.4 %copy.14 = bf16[1,128,4096]{2,1,0:T(8,128)(2,1)} copy(bf16[1,128,4096]{2,1,0:T(8,128)(2,1)} %bitcast.16) | data formatting | bytes 2097152
  213.5 0.0 slice-start.1
  213.5 5.2 %copy.15 = f32[3,192,2048]{2,1,0:T(8,128)} copy(f32[3,192,2048]{2,1,0:T(8,128)} %bitcast.12) | data formatting | bytes 9437184
  218.7 0.0 slice-done
  218.7 0.0 slice-done.1
  218.7 2.2 copy.16
  (1 shorter events, 0.0 us)
Async XLA Ops:
  211.1 7.6 %slice-start = ((s8[4718592]{0:T(1024)(128)(4,1)}), s8[4194304]{0:T(1024)(128)(4,1)S(1)}, s32[]{:S(2)}) async-start(s8[4718592]{0:T(1024)(128)(4,1)} %bitcast.9), calls=%async_computation | async-start | bytes 8388608
  213.5 5.2 %slice-start.1 = ((s8[4718592]{0:T(1024)(128)(4,1)}), s8[524288]{0:T(1024)(128)(4,1)S(1)}, s32[]{:S(2)}) async-start(s8[4718592]{0:T(1024)(128)(4,1)} %bitcast.9), calls=%async_computation.1 | async-start | bytes 1048576

commit v2 on v1

--- a/solution.py
+++ b/solution.py
@@ -20,16 +20,112 @@
 PARTS = 4
 PART = HALF // PARTS
 BLOCK = 256
-ORDER = (("g", 0), ("g", 1), ("d", 0), ("d", 1), ("g", 2), ("d", 2), ("d", 3))
-STEPS = len(ORDER)
-AHEAD = 2
+GATES = 3
+STEPS = [("g", n) for n in range(GATES)] + [("d", n) for n in range(PARTS)]
+
+SCHEDULE = (
+    ("start_rs", "d", 2),
+    ("start_rs", "d", 1),
+    ("pack",),
+    ("scatter", 1),
+    ("dispatch", 0),
+    ("scatter", 4),
+    ("scatter", 7),
+    ("scatter", 8),
+    ("start_rs", "g", 2),
+    ("scatter", 2),
+    ("scatter", 3),
+    ("scatter", 10),
+    ("update", "d", 2),
+    ("dispatch", 2),
+    ("start_rs", "d", 0),
+    ("scatter", 0),
+    ("dispatch", 5),
+    ("dispatch", 1),
+    ("scatter", 9),
+    ("dispatch", 4),
+    ("scatter", 5),
+    ("start_rs", "g", 1),
+    ("x_forward", 1),
+    ("d_send", 2, 0),
+    ("update", "d", 1),
+    ("scatter", 6),
+    ("x_forward", 2),
+    ("dispatch", 3),
+    ("update", "g", 2),
+    ("gathered", "d", 2),
+    ("start_rs", "g", 0),
+    ("dispatch", 6),
+    ("d_send", 2, 1),
+    ("d_send", 1, 0),
+    ("dispatch", 7),
+    ("x_forward", 4),
+    ("x_forward", 0),
+    ("d_near", 2, 1, 1),
+    ("start_rs", "d", 3),
+    ("gathered", "d", 1),
+    ("x_forward", 6),
+    ("x_forward", 3),
+    ("d_far", 2, 1),
+    ("x_forward", 5),
+    ("update", "g", 1),
+    ("update", "d", 0),
+    ("d_send", 1, 1),
+    ("update", "g", 0),
+    ("d_near", 2, 0, 0),
+    ("x_forward", 7),
+    ("d_send", 0, 0),
+    ("gathered", "g", 2),
+    ("d_near", 1, 1, 1),
+    ("d_far", 2, 0),
+    ("d_near", 1, 0, 0),
+    ("d_near", 2, 0, 1),
+    ("d_near", 1, 0, 1),
+    ("gathered", "g", 1),
+    ("update", "d", 3),
+    ("d_near", 1, 1, 0),
+    ("gathered", "d", 0),
+    ("x_rest",),
+    ("d_send", 3, 0),
+    ("d_send", 0, 1),
+    ("hidden", 2),
+    ("d_near", 2, 1, 0),
+    ("d_far", 1, 1),
+    ("d_far", 1, 0),
+    ("hidden", 1),
+    ("gathered", "g", 0),
+    ("d_near", 0, 0, 1),
+    ("hidden", 0),
+    ("d_near", 0, 0, 0),
+    ("gathered", "d", 3),
+    ("d_near", 0, 1, 0),
+    ("d_send", 3, 1),
+    ("d_near", 0, 1, 1),
+    ("hidden_rest",),
+    ("project", 2),
+    ("project", 1),
+    ("d_far", 0, 0),
+    ("d_near", 3, 1, 1),
+    ("d_near", 3, 0, 0),
+    ("d_far", 0, 1),
+    ("d_near", 3, 0, 1),
+    ("d_near", 3, 1, 0),
+    ("project", 0),
+    ("d_far", 3, 0),
+    ("d_far", 3, 1),
+    ("project", 3),
+    ("finish", 0),
+    ("finish", 1),
+    ("finish", 2),
+    ("finish", 3),
+)
 
 
 def kernel(
-    tok, ids, rw, inner, outer, mom, eo, no, nm,
-    tokv, packed, xs, wg, wd, rg, rd, og, od, ob, mb, hs, hid, ys, ret, eov, place,
-    s_rs, r_rs, s_ag, r_ag, l_in, l_out, s_sg, r_sg, s_dz, r_dz, s_df, r_df, s_sd, r_sd,
-    s_dp, r_dp, s_xz, r_xz, s_xf, r_xf, s_h, r_h, s_rt, r_rt, l_rt, l_eo, l_tok,
+    tok, ids, rw, inner, outer, mom, eov, ob, mb,
+    tokv, packed, xs, wg, wd, rg, rd, og, od, hs, hid, ys, ret, place, weight,
+    s_rs, r_rs, s_ag, r_ag, l_in, s_sg, r_sg, s_dz, r_dz, s_df, r_df, s_sd, r_sd,
+    s_dp, r_dp, s_xz, r_xz, s_xf, r_xf, s_h, r_h, s_rt, r_rt, l_tok,
 ):
     g = lax.axis_index("group")
     e = lax.axis_index("expert")
@@ -58,7 +154,6 @@
         pl.semaphore_signal(barrier, inc=1, device_id=other, device_id_type=MESH)
 
     sends = []
-    locals_ = []
 
     def send(src, dst, ss, rs, dev):
         copy = pltpu.make_async_remote_copy(
@@ -82,13 +177,13 @@
     half_of = (mine, theirs)
 
     def in_view(ref, step, offset):
-        kind, n = ORDER[step]
+        kind, n = STEPS[step]
         if kind == "g":
             return ref.at[0:2, n, :, pl.ds(offset, HALF)]
         return ref.at[2, :, :, pl.ds(offset + n * PART, PART)]
 
     def half_view(ref_g, ref_d, step):
-        kind, n = ORDER[step]
+        kind, n = STEPS[step]
         if kind == "g":
             return ref_g.at[n]
         return ref_d.at[:, :, pl.ds(n * PART, PART)]
@@ -100,12 +195,12 @@
         return wd.at[zz, :, core, :, pl.ds(half_of[kind] + n * PART, PART)]
 
     def fresh_view(step, kind):
-        name, n = ORDER[step]
+        name, n = STEPS[step]
         return wg_view(n, kind, c) if name == "g" else wd_view(n, kind, z, c)
 
     tok_copy = local(tok, tokv, l_tok)
     loads = []
-    for step in range(STEPS):
+    for step in range(len(STEPS)):
         loads.append(
             (
                 local(in_view(inner, step, mine), half_view(og, od, step), l_in.at[step, 0]),
@@ -114,36 +209,36 @@
             )
         )
 
-    lane = lax.broadcasted_iota(jnp.int32, (128, 128), 1)
-    row = lax.broadcasted_iota(jnp.int32, (128, 128), 0)
-    named = ids[...]
-    one_hot = (lane == named).astype(F32)
-    earlier = (lane < row).astype(F32)
-    rank = jnp.dot(earlier.astype(BF16), one_hot.astype(BF16), preferred_element_type=F32)
-    rank = jnp.sum(rank * one_hot, axis=1, keepdims=True)
-    slot = named.astype(F32) * CAP + rank
-    wide = lax.broadcasted_iota(jnp.int32, (128, BLOCK), 1).astype(F32)
-    placing = (wide == slot).astype(F32)
-    place[...] = placing.astype(BF16)
-    pack = jnp.transpose(placing).astype(BF16)
-    tok_copy.wait()
-
-    @pl.loop(0, WIDTH // 512)
-    def _(n):
-        cols = pl.ds(pl.multiple_of(n * 512, 512), 512)
-        packed[:, cols] = jnp.dot(pack, tokv[:, cols], preferred_element_type=F32).astype(BF16)
-
-    pl.semaphore_wait(barrier, len(near))
-
-    def start_rs(step):
-        if step < STEPS:
-            send(
-                in_view(inner, step, theirs), half_view(rg, rd, step),
-                s_rs.at[step], r_rs.at[step], partner,
-            )
-
-    for step in range(AHEAD):
-        start_rs(step)
+    def pack():
+        lane = lax.broadcasted_iota(jnp.int32, (128, 128), 1)
+        row = lax.broadcasted_iota(jnp.int32, (128, 128), 0)
+        named = ids[...]
+        one_hot = (row == named).astype(F32)
+        earlier = (row < lane).astype(BF16)
+        rank = jnp.dot(one_hot.astype(BF16), earlier, preferred_element_type=F32)
+        rank = jnp.sum(rank * one_hot, axis=0, keepdims=True)
+        slot = named.astype(F32) * CAP + rank
+        tall = lax.broadcasted_iota(jnp.int32, (BLOCK, 128), 0).astype(F32)
+        placing = (tall == slot).astype(F32)
+        place[...] = jnp.transpose(placing).astype(BF16)
+        weight[...] = jnp.sum(jnp.where(lane == row, rw[...], 0.0), axis=1, keepdims=True)
+        tok_copy.wait()
+
+        @pl.loop(0, WIDTH // 512)
+        def _(n):
+            cols = pl.ds(pl.multiple_of(n * 512, 512), 512)
+            packed[:, cols] = jnp.dot(
+                placing.astype(BF16), tokv[:, cols], preferred_element_type=F32
+            ).astype(BF16)
+
+        xs[z, rows_at(y * 32, 32), :] = packed[expert_rows(0, y, 0, 32), :]
+
+    def start_rs(name, n):
+        step = STEPS.index((name, n))
+        send(
+            in_view(inner, step, theirs), half_view(rg, rd, step),
+            s_rs.at[step], r_rs.at[step], partner,
+        )
 
     def rows_at(start, size):
         return pl.ds(pl.multiple_of(start, 16), size)
@@ -162,8 +257,7 @@
     def buffer_rows(s, yy, first, size):
         return rows_at((0 if s == 0 else 128) + yy * 32 + first, size)
 
-    xs[z, rows_at(y * 32, 32), :] = packed[expert_rows(0, y, 0, 32), :]
-    for n in (0, 3, 7, 2, 4, 8, 6, 10, 1, 5, 9):
+    def scatter(n):
         s, dy, first, size = spread(n)
         send(
             packed.at[expert_rows(s, turn(y, dy), first, size)],
@@ -205,18 +299,21 @@
         new_m = momentum_rate * m + pseudo
         return o - outer_rate * (pseudo + momentum_rate * new_m), new_m
 
-    def share(step, kind):
-        name, n = ORDER[step]
+    def share(name, n, kind):
+        step = STEPS.index((name, n))
         view = fresh_view(step, kind)
         if name == "g":
             send(view, view, s_sg.at[n, kind], r_sg.at[n, kind], sibling)
         else:
-            send(view, view, s_dz.at[n, kind, 0], r_dz.at[n, kind, 0], up)
-            send(view, view, s_dz.at[n, kind, 1], r_dz.at[n, kind, 1], down)
             send(view, view, s_sd.at[n, kind, 0], r_sd.at[n, kind, 0], sibling)
 
-    def update(step):
-        name, n = ORDER[step]
+    def d_send(n, kind):
+        view = wd_view(n, kind, z, c)
+        send(view, view, s_dz.at[n, kind, 0], r_dz.at[n, kind, 0], up)
+        send(view, view, s_dz.at[n, kind, 1], r_dz.at[n, kind, 1], down)
+
+    def update(name, n):
+        step = STEPS.index((name, n))
         for copy in loads[step]:
             copy.wait()
         arrived(half_view(rg, rd, step), s_rs.at[step], r_rs.at[step])
@@ -241,22 +338,19 @@
 
         view = fresh_view(step, 0)
         send(view, view, s_ag.at[step], r_ag.at[step], partner)
-        start_rs(step + AHEAD)
-        share(step, 0)
-        locals_.append(local(in_view(ob, step, 0), in_view(no, step, 0), l_out.at[step, 0]))
-        locals_.append(local(in_view(mb, step, 0), in_view(nm, step, 0), l_out.at[step, 1]))
-
-    def gathered(step):
+        share(name, n, 0)
+
+    def gathered(name, n):
+        step = STEPS.index((name, n))
         arrived(fresh_view(step, 1), s_ag.at[step], r_ag.at[step])
-        share(step, 1)
-
-    def d_near(n, kind):
-        for way in (0, 1):
-            view = wd_view(n, kind, turn(z, 1 if way else 3), c)
-            arrived(view, s_dz.at[n, kind, way], r_dz.at[n, kind, way])
-            if way == kind:
-                send(view, view, s_df.at[n, kind], r_df.at[n, kind], down if way else up)
-            send(view, view, s_sd.at[n, kind, 1 + way], r_sd.at[n, kind, 1 + way], sibling)
+        share(name, n, 1)
+
+    def d_near(n, kind, way):
+        view = wd_view(n, kind, turn(z, 1 if way else 3), c)
+        arrived(view, s_dz.at[n, kind, way], r_dz.at[n, kind, way])
+        if way == kind:
+            send(view, view, s_df.at[n, kind], r_df.at[n, kind], down if way else up)
+        send(view, view, s_sd.at[n, kind, 1 + way], r_sd.at[n, kind, 1 + way], sibling)
 
     def d_far(n, kind):
         view = wd_view(n, kind, turn(z, 2), c)
@@ -322,7 +416,7 @@
                 ).astype(BF16)
 
         cols = pl.ds(n * PART, PART)
-        for m in range(11):
+        for m in (0, 3, 7, 2, 4, 8, 6, 10, 1, 5, 9):
             s, dy, first, size = spread(m)
             back = xn[(0, 2, 1)[s]]
             send(
@@ -343,70 +437,19 @@
         for h in (0, 1):
             picked = jnp.dot(place[...], ret[h, :, cols], preferred_element_type=F32)
             wide_cols = pl.ds(h * HALF + n * PART, PART)
-            eov[:, wide_cols] = (rw[...] * picked).astype(BF16)
-            locals_.append(local(eov.at[:, wide_cols], eo.at[:, wide_cols], l_eo.at[n, h]))
-
-    dispatch(0)
-    for p in (1, 4, 5, 3):
-        dispatch(p)
-    update(0)
-    for p in (7, 2, 6):
-        dispatch(p)
-    x_forward(0)
-    x_forward(1)
-    x_forward(4)
-    update(1)
-    x_forward(5)
-    x_forward(3)
-    gathered(0)
-    update(2)
-    x_forward(7)
-    x_forward(2)
-    x_forward(6)
-    gathered(1)
-    update(3)
-    gathered(2)
-    x_rest()
-    hidden(0)
-    update(4)
-    gathered(3)
-    hidden(1)
-    update(5)
-    d_near(0, 0)
-    d_near(0, 1)
-    gathered(4)
-    d_far(0, 0)
-    d_far(0, 1)
-    d_near(1, 0)
-    d_near(1, 1)
-    hidden(2)
-    update(6)
-    gathered(5)
-    d_far(1, 0)
-    d_far(1, 1)
-    gathered(6)
-    hidden_rest()
-    project(0)
-    d_near(2, 0)
-    d_near(2, 1)
-    project(1)
-    d_far(2, 0)
-    d_far(2, 1)
-    d_near(3, 0)
-    d_near(3, 1)
-    project(2)
-    finish(0)
-    d_far(3, 0)
-    d_far(3, 1)
-    finish(1)
-    project(3)
-    finish(2)
-    finish(3)
+            eov[:, wide_cols] = (weight[...] * picked).astype(BF16)
+
+    pl.semaphore_wait(barrier, len(near))
+    actions = (
+        pack, start_rs, scatter, dispatch, x_forward, x_rest, update, gathered, d_send, d_near,
+        d_far, hidden, hidden_rest, project, finish,
+    )
+    actions = {action.__name__: action for action in actions}
+    for name, *parts in SCHEDULE:
+        actions[name](*parts)
 
     for copy in sends:
         copy.wait_send()
-    for copy in locals_:
-        copy.wait()
 
 
 def per_device(tokens, expert_ids, route_weight, inner_weights, outer_weights, momentum):
@@ -425,17 +468,15 @@
         vmem((3, 64, HALF), BF16),
         vmem((3, 2, 64, HALF), BF16),
         vmem((3, 64, HALF), BF16),
-        vmem(weights, F32),
-        vmem(weights, F32),
         vmem((3, 4, BLOCK, 128), BF16),
         vmem((BLOCK, 1536), BF16),
         vmem((2, BLOCK, HALF), BF16),
         vmem((2, BLOCK, HALF), BF16),
-        vmem((128, WIDTH), BF16),
         vmem((128, BLOCK), BF16),
+        vmem((128, 1), F32),
     ]
-    scratch += [dma((STEPS,))] * 4
-    scratch += [dma((STEPS, 3)), dma((STEPS, 2))]
+    scratch += [dma((len(STEPS),))] * 4
+    scratch += [dma((len(STEPS), 3))]
     scratch += [dma((3, 2))] * 2
     scratch += [dma((PARTS, 2, 2))] * 2
     scratch += [dma((PARTS, 2))] * 2
@@ -445,24 +486,24 @@
     scratch += [dma((8,))] * 2
     scratch += [dma((3, 3))] * 2
     scratch += [dma((PARTS, 11))] * 2
-    scratch += [dma((1,)), dma((PARTS, 2)), dma]
+    scratch += [dma]
     out, new_outer, new_momentum = pl.pallas_call(
         kernel,
         out_shape=(
-            jax.ShapeDtypeStruct((128, WIDTH), BF16),
-            jax.ShapeDtypeStruct(weights, F32),
-            jax.ShapeDtypeStruct(weights, F32),
+            vmem((128, WIDTH), BF16),
+            vmem(weights, F32),
+            vmem(weights, F32),
         ),
         in_specs=[any_space, in_vmem, in_vmem, any_space, any_space, any_space],
-        out_specs=(any_space,) * 3,
+        out_specs=(in_vmem,) * 3,
         scratch_shapes=scratch,
         compiler_params=pltpu.CompilerParams(
-            collective_id=0, has_side_effects=True, vmem_limit_bytes=62 << 20
+            collective_id=0, has_side_effects=True, vmem_limit_bytes=49 << 20
         ),
     )(
         tokens.reshape(128, WIDTH),
-        expert_ids.reshape(128, 1),
-        route_weight.reshape(128, 1),
+        expert_ids.reshape(1, 128),
+        route_weight.reshape(1, 128),
         inner_weights.reshape(3, 3, 64, WIDTH),
         outer_weights.reshape(weights),
         momentum.reshape(weights),

time: 221 us -> 169 us (0.76)
  Pallas kernels: 208 us -> 162 us
  local copies, waits for them, and re-layouts: 12.6 us -> 5.34 us
    pallas_call x1, Pallas kernels: 208 us -> 162 us  [per_device(): pl.pallas_call(kernel, out_shape=(vmem((128, WIDTH), BF16), vmem(weights,...]
    unnamed x7 -> x3, local copies, waits for them, and re-layouts: 9.78 us -> 5.34 us
    reshape x2 -> x0, local copies, waits for them, and re-layouts: 2.78 us -> none  [the longest x1 1.39 us: per_device(): expert_ids.reshape(128, 1)]
where the time goes in v2:
time: 169 us; the launch traced here: 168 us
  Pallas kernels  162 us (96%)
  local copies, waits for them, and re-layouts  5.34 us (3%)
    pallas_call x1, Pallas kernels, per_device(): pl.pallas_call(kernel, out_shape=(vmem((128, WIDTH), BF16), vmem(weights,...  162 us
    unnamed x3, local copies, waits for them, and re-layouts  5.34 us

profile of v2, /device:TPU:1, one launch (start us, length us, event | category | flops | bytes accessed | tf_op | source)
XLA Modules:
  0.0 168.1 jit_solution(16912450124248451203)
XLA Ops:
  0.6 162.1 %shard_map.85 = (bf16[128,4096]{1,0:T(8,128)(2,1)S(1)}, f32[3,3,64,2048]{3,2,1,0:T(8,128)S(1)}, f32[3,3,64,2048]{3,2,1,0:T(8,128)S(1)}) custom-call(bf16[128,4096]{1,0:T(8,128)(2,1)} %bitcast.15, s32[1,128]{1,0:T(1,128)} %bitcast.16, f32[1,128]{1,0:T(1,128)} %bitcast.17, bf16[3,3,64,4096]{3,2,1,0:T(8,128)(2,1)} %bitcast.12, f32[3,3,64,2048]{3,2,1,0:T(8,128)} %bitcast.13, ...), custom_call_target="tpu_custom_call" | custom-call | tf_op jit(solution)/shard_map/pallas_call | solution.py:490
  162.7 1.0 copy.12
  163.7 2.2 %copy.13 = f32[3,192,2048]{2,1,0:T(8,128)} copy(f32[3,192,2048]{2,1,0:T(8,128)S(1)} %bitcast.10) | data formatting | bytes 9437184
  165.9 2.2 %copy.14 = f32[3,192,2048]{2,1,0:T(8,128)} copy(f32[3,192,2048]{2,1,0:T(8,128)S(1)} %bitcast.9) | data formatting | bytes 9437184

commit v3 on v2

--- a/solution.py
+++ b/solution.py
@@ -17,107 +17,107 @@
 WIDTH = 4096
 HALF = 2048
 CAP = 32
-PARTS = 4
-PART = HALF // PARTS
+WIDTHS = (512, 512, 512, 512)
+PARTS = len(WIDTHS)
+STARTS = [sum(WIDTHS[:n]) for n in range(PARTS)]
 BLOCK = 256
 GATES = 3
 STEPS = [("g", n) for n in range(GATES)] + [("d", n) for n in range(PARTS)]
 
 SCHEDULE = (
+    ("start_rs", "d", 1),
+    ("dispatch", 0),
+    ("scatter", 0),
+    ("start_rs", "d", 0),
+    ("start_rs", "d", 3),
+    ("scatter", 7),
+    ("scatter", 2),
+    ("update", "d", 1),
+    ("d_send", 1, 0),
+    ("update", "d", 0),
+    ("d_send", 0, 0),
+    ("dispatch", 1),
+    ("dispatch", 3),
+    ("scatter", 3),
+    ("gathered", "d", 1),
+    ("gathered", "d", 0),
+    ("scatter", 4),
+    ("scatter", 8),
+    ("dispatch", 4),
+    ("scatter", 10),
+    ("d_near", 1, 0, 1),
+    ("d_send", 1, 1),
+    ("update", "d", 3),
+    ("d_send", 0, 1),
+    ("scatter", 6),
+    ("scatter", 9),
+    ("d_send", 3, 0),
+    ("start_rs", "g", 0),
+    ("dispatch", 5),
+    ("scatter", 1),
+    ("d_near", 0, 0, 0),
+    ("x_forward", 4),
+    ("x_forward", 3),
+    ("dispatch", 2),
+    ("start_rs", "g", 1),
+    ("d_near", 0, 1, 1),
+    ("dispatch", 7),
+    ("scatter", 5),
+    ("x_forward", 0),
+    ("update", "g", 0),
+    ("gathered", "d", 3),
+    ("x_forward", 5),
+    ("dispatch", 6),
+    ("d_near", 0, 0, 1),
+    ("start_rs", "g", 2),
+    ("x_forward", 1),
+    ("update", "g", 1),
+    ("gathered", "g", 0),
+    ("d_send", 3, 1),
+    ("x_forward", 2),
+    ("d_near", 1, 0, 0),
+    ("d_near", 3, 0, 1),
+    ("d_near", 3, 0, 0),
+    ("x_forward", 7),
+    ("x_forward", 6),
+    ("update", "g", 2),
+    ("d_far", 0, 1),
+    ("d_near", 3, 1, 1),
+    ("gathered", "g", 1),
+    ("d_near", 1, 1, 1),
+    ("x_rest",),
+    ("d_far", 0, 0),
+    ("hidden", 0),
+    ("hidden", 1),
+    ("gathered", "g", 2),
     ("start_rs", "d", 2),
-    ("start_rs", "d", 1),
-    ("pack",),
-    ("scatter", 1),
-    ("dispatch", 0),
-    ("scatter", 4),
-    ("scatter", 7),
-    ("scatter", 8),
-    ("start_rs", "g", 2),
-    ("scatter", 2),
-    ("scatter", 3),
-    ("scatter", 10),
+    ("d_far", 1, 0),
+    ("d_near", 3, 1, 0),
+    ("d_near", 0, 1, 0),
+    ("d_far", 1, 1),
+    ("hidden", 2),
     ("update", "d", 2),
-    ("dispatch", 2),
-    ("start_rs", "d", 0),
-    ("scatter", 0),
-    ("dispatch", 5),
-    ("dispatch", 1),
-    ("scatter", 9),
-    ("dispatch", 4),
-    ("scatter", 5),
-    ("start_rs", "g", 1),
-    ("x_forward", 1),
     ("d_send", 2, 0),
-    ("update", "d", 1),
-    ("scatter", 6),
-    ("x_forward", 2),
-    ("dispatch", 3),
-    ("update", "g", 2),
+    ("hidden_rest",),
+    ("project", 0),
     ("gathered", "d", 2),
-    ("start_rs", "g", 0),
-    ("dispatch", 6),
+    ("d_near", 1, 1, 0),
+    ("d_far", 3, 0),
     ("d_send", 2, 1),
-    ("d_send", 1, 0),
-    ("dispatch", 7),
-    ("x_forward", 4),
-    ("x_forward", 0),
+    ("d_near", 2, 0, 0),
+    ("d_far", 3, 1),
+    ("project", 1),
     ("d_near", 2, 1, 1),
-    ("start_rs", "d", 3),
-    ("gathered", "d", 1),
-    ("x_forward", 6),
-    ("x_forward", 3),
+    ("project", 3),
+    ("d_near", 2, 0, 1),
+    ("d_near", 2, 1, 0),
+    ("d_far", 2, 0),
     ("d_far", 2, 1),
-    ("x_forward", 5),
-    ("update", "g", 1),
-    ("update", "d", 0),
-    ("d_send", 1, 1),
-    ("update", "g", 0),
-    ("d_near", 2, 0, 0),
-    ("x_forward", 7),
-    ("d_send", 0, 0),
-    ("gathered", "g", 2),
-    ("d_near", 1, 1, 1),
-    ("d_far", 2, 0),
-    ("d_near", 1, 0, 0),
-    ("d_near", 2, 0, 1),
-    ("d_near", 1, 0, 1),
-    ("gathered", "g", 1),
-    ("update", "d", 3),
-    ("d_near", 1, 1, 0),
-    ("gathered", "d", 0),
-    ("x_rest",),
-    ("d_send", 3, 0),
-    ("d_send", 0, 1),
-    ("hidden", 2),
-    ("d_near", 2, 1, 0),
-    ("d_far", 1, 1),
-    ("d_far", 1, 0),
-    ("hidden", 1),
-    ("gathered", "g", 0),
-    ("d_near", 0, 0, 1),
-    ("hidden", 0),
-    ("d_near", 0, 0, 0),
-    ("gathered", "d", 3),
-    ("d_near", 0, 1, 0),
-    ("d_send", 3, 1),
-    ("d_near", 0, 1, 1),
-    ("hidden_rest",),
     ("project", 2),
-    ("project", 1),
-    ("d_far", 0, 0),
-    ("d_near", 3, 1, 1),
-    ("d_near", 3, 0, 0),
-    ("d_far", 0, 1),
-    ("d_near", 3, 0, 1),
-    ("d_near", 3, 1, 0),
-    ("project", 0),
-    ("d_far", 3, 0),
-    ("d_far", 3, 1),
-    ("project", 3),
+    ("finish", 3),
+    ("finish", 1),
     ("finish", 0),
-    ("finish", 1),
     ("finish", 2),
-    ("finish", 3),
 )
 
 
@@ -141,15 +141,20 @@
     def turn(a, n):
         return lax.rem(a + n, 4)
 
-    partner = device(turn(x, 2), y, z, c)
+    def around(a):
+        way = 1 + 2 * lax.rem(a, 2)
+        return a, turn(a, way), turn(a, 2), turn(a, 4 - way)
+
+    ring, yn, zn = around(x), around(y), around(z)
+    xn = (ring[0], ring[1], ring[3])
+    partner = device(ring[2], y, z, c)
     sibling = device(x, y, z, 1 - c)
-    up, down, far = (device(x, y, turn(z, n), c) for n in (1, 3, 2))
-    xn = (x, turn(x, 1), turn(x, 3))
+    zdev = [device(x, y, zz, c) for zz in zn]
 
     barrier = pltpu.get_barrier_semaphore()
-    near = [partner, sibling, up, down, far]
-    near += [device(x, turn(y, dy), z, c) for dy in (1, 2, 3)]
-    near += [device(xn[s], turn(y, dy), z, c) for s in (1, 2) for dy in range(4)]
+    near = [partner, sibling] + zdev[1:]
+    near += [device(x, yn[k], z, c) for k in (1, 2, 3)]
+    near += [device(xn[s], yn[k], z, c) for s in (1, 2) for k in range(4)]
     for other in near:
         pl.semaphore_signal(barrier, inc=1, device_id=other, device_id_type=MESH)
 
@@ -180,34 +185,34 @@
         kind, n = STEPS[step]
         if kind == "g":
             return ref.at[0:2, n, :, pl.ds(offset, HALF)]
-        return ref.at[2, :, :, pl.ds(offset + n * PART, PART)]
+        return ref.at[2, :, :, pl.ds(offset + STARTS[n], WIDTHS[n])]
 
     def half_view(ref_g, ref_d, step):
         kind, n = STEPS[step]
         if kind == "g":
             return ref_g.at[n]
-        return ref_d.at[:, :, pl.ds(n * PART, PART)]
+        return ref_d.at[:, :, pl.ds(STARTS[n], WIDTHS[n])]
 
     def wg_view(n, kind, core):
         return wg.at[n, :, core, :, pl.ds(half_of[kind], HALF)]
 
     def wd_view(n, kind, zz, core):
-        return wd.at[zz, :, core, :, pl.ds(half_of[kind] + n * PART, PART)]
+        return wd.at[zz, :, core, :, pl.ds(half_of[kind] + STARTS[n], WIDTHS[n])]
 
     def fresh_view(step, kind):
         name, n = STEPS[step]
         return wg_view(n, kind, c) if name == "g" else wd_view(n, kind, z, c)
 
     tok_copy = local(tok, tokv, l_tok)
-    loads = []
-    for step in range(len(STEPS)):
-        loads.append(
-            (
+    loads = {}
+    for name, *part in SCHEDULE:
+        if name == "update":
+            step = STEPS.index(tuple(part))
+            loads[step] = (
                 local(in_view(inner, step, mine), half_view(og, od, step), l_in.at[step, 0]),
                 local(in_view(outer, step, 0), in_view(ob, step, 0), l_in.at[step, 1]),
                 local(in_view(mom, step, 0), in_view(mb, step, 0), l_in.at[step, 2]),
             )
-        )
 
     def pack():
         lane = lax.broadcasted_iota(jnp.int32, (128, 128), 1)
@@ -258,41 +263,38 @@
         return rows_at((0 if s == 0 else 128) + yy * 32 + first, size)
 
     def scatter(n):
-        s, dy, first, size = spread(n)
+        s, k, first, size = spread(n)
         send(
-            packed.at[expert_rows(s, turn(y, dy), first, size)],
+            packed.at[expert_rows(s, yn[k], first, size)],
             xs.at[z, buffer_rows(s, y, first, size)],
-            s_dp.at[n], r_dp.at[n], device(xn[s], turn(y, dy), z, c),
+            s_dp.at[n], r_dp.at[n], device(xn[s], yn[k], z, c),
         )
 
     def x_piece(zz, p):
-        s, dy = p // 4, p % 4
-        return xs.at[zz, buffer_rows(s, turn(y, 4 - dy), 0, 32)]
+        return xs.at[zz, buffer_rows(p // 4, yn[p % 4], 0, 32)]
 
     def dispatch(p):
-        s, dy = p // 4, p % 4
-        for n in ((dy - 1,) if s == 0 else (3 + dy, 7 + dy)):
+        k = p % 4
+        for n in ((k - 1,) if p < 4 else (3 + k, 7 + k)):
             if n >= 0:
-                sn, _, first, size = spread(n)
-                arrived(
-                    xs.at[z, buffer_rows(sn, turn(y, 4 - dy), first, size)], s_dp.at[n], r_dp.at[n]
-                )
+                s, _, first, size = spread(n)
+                arrived(xs.at[z, buffer_rows(s, yn[k], first, size)], s_dp.at[n], r_dp.at[n])
         view = x_piece(z, p)
-        send(view, view, s_xz.at[p, 0], r_xz.at[p, 0], up)
-        send(view, view, s_xz.at[p, 1], r_xz.at[p, 1], down)
+        send(view, view, s_xz.at[p, 0], r_xz.at[p, 0], zdev[1])
+        send(view, view, s_xz.at[p, 1], r_xz.at[p, 1], zdev[3])
 
     def x_forward(p):
         way = p // 4
-        view = x_piece(turn(z, 1 if way else 3), p)
+        view = x_piece(zn[3 if way else 1], p)
         arrived(view, s_xz.at[p, way], r_xz.at[p, way])
-        send(view, view, s_xf.at[p], r_xf.at[p], down if way else up)
+        send(view, view, s_xf.at[p], r_xf.at[p], zdev[1 if way else 3])
 
     def x_rest():
         for p in range(8):
             way = 1 - p // 4
-            arrived(x_piece(turn(z, 1 if way else 3), p), s_xz.at[p, way], r_xz.at[p, way])
+            arrived(x_piece(zn[3 if way else 1], p), s_xz.at[p, way], r_xz.at[p, way])
         for p in range(8):
-            arrived(x_piece(turn(z, 2), p), s_xf.at[p], r_xf.at[p])
+            arrived(x_piece(zn[2], p), s_xf.at[p], r_xf.at[p])
 
     def outer_step(o, m, a, b):
         pseudo = o - (a.astype(F32) + b.astype(F32)) / 2
@@ -309,8 +311,8 @@
 
     def d_send(n, kind):
         view = wd_view(n, kind, z, c)
-        send(view, view, s_dz.at[n, kind, 0], r_dz.at[n, kind, 0], up)
-        send(view, view, s_dz.at[n, kind, 1], r_dz.at[n, kind, 1], down)
+        send(view, view, s_dz.at[n, kind, 0], r_dz.at[n, kind, 0], zdev[1])
+        send(view, view, s_dz.at[n, kind, 1], r_dz.at[n, kind, 1], zdev[3])
 
     def update(name, n):
         step = STEPS.index((name, n))
@@ -326,15 +328,15 @@
                     at = (i, n, rows, slice(None))
                     a, b = og[n, i, rows, :], rg[n, i, rows, :]
                 else:
-                    at = (2, i, rows, pl.ds(n * PART, PART))
-                    a, b = od[i, rows, pl.ds(n * PART, PART)], rd[i, rows, pl.ds(n * PART, PART)]
+                    at = (2, i, rows, pl.ds(STARTS[n], WIDTHS[n]))
+                    a, b = od[i, rows, pl.ds(STARTS[n], WIDTHS[n])], rd[i, rows, pl.ds(STARTS[n], WIDTHS[n])]
                 new_o, new_m = outer_step(ob[at], mb[at], a, b)
                 ob[at] = new_o
                 mb[at] = new_m
                 if name == "g":
                     wg[n, i, c, rows, pl.ds(mine, HALF)] = new_o.astype(BF16)
                 else:
-                    wd[z, i, c, rows, pl.ds(mine + n * PART, PART)] = new_o.astype(BF16)
+                    wd[z, i, c, rows, pl.ds(mine + STARTS[n], WIDTHS[n])] = new_o.astype(BF16)
 
         view = fresh_view(step, 0)
         send(view, view, s_ag.at[step], r_ag.at[step], partner)
@@ -346,14 +348,14 @@
         share(name, n, 1)
 
     def d_near(n, kind, way):
-        view = wd_view(n, kind, turn(z, 1 if way else 3), c)
+        view = wd_view(n, kind, zn[3 if way else 1], c)
         arrived(view, s_dz.at[n, kind, way], r_dz.at[n, kind, way])
         if way == kind:
-            send(view, view, s_df.at[n, kind], r_df.at[n, kind], down if way else up)
+            send(view, view, s_df.at[n, kind], r_df.at[n, kind], zdev[1 if way else 3])
         send(view, view, s_sd.at[n, kind, 1 + way], r_sd.at[n, kind, 1 + way], sibling)
 
     def d_far(n, kind):
-        view = wd_view(n, kind, turn(z, 2), c)
+        view = wd_view(n, kind, zn[2], c)
         arrived(view, s_df.at[n, kind], r_df.at[n, kind])
         send(view, view, s_sd.at[n, kind, 3], r_sd.at[n, kind, 3], sibling)
 
@@ -366,7 +368,7 @@
 
         @pl.loop(0, 4)
         def _(r):
-            zz = turn(z, r + 1)
+            zz = turn(z, (r + 1) * (1 + 2 * lax.rem(z, 2)))
             both = lax.dot_general(
                 xs[zz], wg[n].reshape(256, WIDTH), (((1,), (1,)), ((), ())),
                 preferred_element_type=F32,
@@ -389,59 +391,59 @@
                 pltpu.make_async_remote_copy(
                     src_ref=hs.at[n, r], dst_ref=hid.at[:, hid_cols(z, n)],
                     send_sem=s_h.at[n, r], recv_sem=r_h.at[n, r],
-                    device_id=device(x, y, turn(z, r + 1), c), device_id_type=MESH,
+                    device_id=zdev[r + 1], device_id_type=MESH,
                 )
             )
 
     def hidden_rest():
         for n in range(3):
             for r in range(3):
-                arrived(hid.at[:, hid_cols(turn(z, 3 - r), n)], s_h.at[n, r], r_h.at[n, r])
+                arrived(hid.at[:, hid_cols(zn[r + 1], n)], s_h.at[n, r], r_h.at[n, r])
 
     def project(n):
         for kind in (0, 1):
-            for k, dz in enumerate((0, 3, 1, 2)):
+            for k, near_z in enumerate((0, 1, 3, 2)):
                 arrived(
-                    wd_view(n, kind, turn(z, dz), 1 - c), s_sd.at[n, kind, k], r_sd.at[n, kind, k]
+                    wd_view(n, kind, zn[near_z], 1 - c), s_sd.at[n, kind, k], r_sd.at[n, kind, k]
                 )
         for h in (0, 1):
 
-            @pl.loop(0, PART // 256)
+            @pl.loop(0, WIDTHS[n] // 256)
             def _(t):
-                cols = pl.ds(pl.multiple_of(n * PART + t * 256, 256), 256)
-                wide_cols = pl.ds(pl.multiple_of(h * HALF + n * PART + t * 256, 256), 256)
+                cols = pl.ds(pl.multiple_of(STARTS[n] + t * 256, 256), 256)
+                wide_cols = pl.ds(pl.multiple_of(h * HALF + STARTS[n] + t * 256, 256), 256)
                 ys[h, :, cols] = jnp.dot(
                     hid[...], wd[:, :, :, :, wide_cols].reshape(1536, 256),
                     preferred_element_type=F32,
                 ).astype(BF16)
 
-        cols = pl.ds(n * PART, PART)
-        for m in (0, 3, 7, 2, 4, 8, 6, 10, 1, 5, 9):
-            s, dy, first, size = spread(m)
-            back = xn[(0, 2, 1)[s]]
+        cols = pl.ds(STARTS[n], WIDTHS[n])
+        for m in (1, 8, 4, 0, 5, 9, 2, 6, 10, 3, 7):
+            s, k, first, size = spread(m)
             send(
-                ys.at[:, buffer_rows(s, turn(y, 4 - dy), first, size), cols],
+                ys.at[:, buffer_rows(s, yn[k], first, size), cols],
                 ret.at[:, rows_at((low * 4 + y) * CAP + first, size), cols],
-                s_rt.at[n, m], r_rt.at[n, m], device(back, turn(y, 4 - dy), z, c),
+                s_rt.at[n, m], r_rt.at[n, m], device(xn[s], yn[k], z, c),
             )
         ret[:, expert_rows(0, y, 0, 32), cols] = ys[:, buffer_rows(0, y, 0, 32), cols]
 
     def finish(n):
-        cols = pl.ds(n * PART, PART)
+        cols = pl.ds(STARTS[n], WIDTHS[n])
         for m in range(11):
-            s, dy, first, size = spread(m)
+            s, k, first, size = spread(m)
             arrived(
-                ret.at[:, expert_rows(s, turn(y, dy), first, size), cols],
+                ret.at[:, expert_rows(s, yn[k], first, size), cols],
                 s_rt.at[n, m], r_rt.at[n, m],
             )
         for h in (0, 1):
             picked = jnp.dot(place[...], ret[h, :, cols], preferred_element_type=F32)
-            wide_cols = pl.ds(h * HALF + n * PART, PART)
+            wide_cols = pl.ds(h * HALF + STARTS[n], WIDTHS[n])
             eov[:, wide_cols] = (weight[...] * picked).astype(BF16)
 
+    pack()
     pl.semaphore_wait(barrier, len(near))
     actions = (
-        pack, start_rs, scatter, dispatch, x_forward, x_rest, update, gathered, d_send, d_near,
+        start_rs, scatter, dispatch, x_forward, x_rest, update, gathered, d_send, d_near,
         d_far, hidden, hidden_rest, project, finish,
     )
     actions = {action.__name__: action for action in actions}
@@ -450,6 +452,17 @@
 
     for copy in sends:
         copy.wait_send()
+
+
+def store(eov, ob, mb, eo, no, nm, sem):
+    copies = [pltpu.make_async_copy(eov, eo, sem.at[0])]
+    for m in range(3):
+        copies.append(pltpu.make_async_copy(ob.at[m], no.at[m], sem.at[1 + m]))
+        copies.append(pltpu.make_async_copy(mb.at[m], nm.at[m], sem.at[4 + m]))
+    for copy in copies:
+        copy.start()
+    for copy in copies:
+        copy.wait()
 
 
 def per_device(tokens, expert_ids, route_weight, inner_weights, outer_weights, momentum):
@@ -508,6 +521,18 @@
         outer_weights.reshape(weights),
         momentum.reshape(weights),
     )
+    out, new_outer, new_momentum = pl.pallas_call(
+        store,
+        out_shape=(
+            jax.ShapeDtypeStruct((128, WIDTH), BF16),
+            jax.ShapeDtypeStruct(weights, F32),
+            jax.ShapeDtypeStruct(weights, F32),
+        ),
+        in_specs=[in_vmem] * 3,
+        out_specs=(any_space,) * 3,
+        scratch_shapes=[dma((7,))],
+        compiler_params=pltpu.CompilerParams(vmem_limit_bytes=40 << 20),
+    )(out, new_outer, new_momentum)
     full = (3, 192, HALF)
     return out[None], new_outer.reshape(full), new_momentum.reshape(full)
 

time: 169 us -> 163 us (0.964)
  local copies, waits for them, and re-layouts: 5.34 us -> 0 us
    unnamed x3 -> x0, local copies, waits for them, and re-layouts: 5.34 us -> none
    pallas_call x0 -> x1, Pallas kernels: none -> 4.01 us  [per_device(): pl.pallas_call(store, out_shape=(jax.ShapeDtypeStruct((128, WIDTH), BF16)...]
    pallas_call x1, Pallas kernels: 162 us -> 158 us  [per_device(): pl.pallas_call(kernel, out_shape=(vmem((128, WIDTH), BF16), vmem(weights,...]
where the time goes in v3:
time: 163 us
  Pallas kernels  162 us (99%)
    pallas_call x1, Pallas kernels, per_device(): pl.pallas_call(kernel, out_shape=(vmem((128, WIDTH), BF16), vmem(weights,...  158 us
    pallas_call x1, Pallas kernels, per_device(): pl.pallas_call(store, out_shape=(jax.ShapeDtypeStruct((128, WIDTH), BF16)...  4.01 us

profile of v3, /device:TPU:1, one launch (start us, length us, event | category | flops | bytes accessed | tf_op | source)
XLA Modules:
  0.0 162.7 jit_solution(2835405361791798278)
XLA Ops:
  0.6 158.1 %shard_map.85 = (bf16[128,4096]{1,0:T(8,128)(2,1)S(1)}, f32[3,3,64,2048]{3,2,1,0:T(8,128)S(1)}, f32[3,3,64,2048]{3,2,1,0:T(8,128)S(1)}) custom-call(bf16[128,4096]{1,0:T(8,128)(2,1)} %bitcast.12, s32[1,128]{1,0:T(1,128)} %bitcast.13, f32[1,128]{1,0:T(1,128)} %bitcast.14, bf16[3,3,64,4096]{3,2,1,0:T(8,128)(2,1)} %bitcast.9, f32[3,3,64,2048]{3,2,1,0:T(8,128)} %bitcast.10, ...), custom_call_target="tpu_custom_call" | custom-call | tf_op jit(solution)/shard_map/pallas_call | solution.py:503
  158.7 4.0 %shard_map.86 = (bf16[128,4096]{1,0:T(8,128)(2,1)}, f32[3,3,64,2048]{3,2,1,0:T(8,128)}, f32[3,3,64,2048]{3,2,1,0:T(8,128)}) custom-call(bf16[128,4096]{1,0:T(8,128)(2,1)S(1)} %get-tuple-element.9.eov, f32[3,3,64,2048]{3,2,1,0:T(8,128)S(1)} %get-tuple-element.10.ob, f32[3,3,64,2048]{3,2,1,0:T(8,128)S(1)} %get-tuple-element.11.mb), custom_call_target="tpu_custom_call" | custom-call | tf_op jit(solution)/shard_map/pallas_call | solution.py:524

commit v4 on v3

--- a/solution.py
+++ b/solution.py
@@ -447,11 +447,12 @@
         d_far, hidden, hidden_rest, project, finish,
     )
     actions = {action.__name__: action for action in actions}
-    for name, *parts in SCHEDULE:
+    for name, *parts in SCHEDULE[:-1]:
         actions[name](*parts)
-
     for copy in sends:
         copy.wait_send()
+    name, *parts = SCHEDULE[-1]
+    actions[name](*parts)
 
 
 def store(eov, ob, mb, eo, no, nm, sem):

time: 163 us -> 163 us (level)
  no operation moved by 1% of the time
where the time goes in v4:
time: 163 us; the launch traced here: 162 us
  Pallas kernels  162 us (99%)
    pallas_call x1, Pallas kernels, per_device(): pl.pallas_call(kernel, out_shape=(vmem((128, WIDTH), BF16), vmem(weights,...  158 us
    pallas_call x1, Pallas kernels, per_device(): pl.pallas_call(store, out_shape=(jax.ShapeDtypeStruct((128, WIDTH), BF16)...  4.01 us

profile of v4, /device:TPU:1, one launch (start us, length us, event | category | flops | bytes accessed | tf_op | source)
XLA Modules:
  0.0 162.5 jit_solution(5042608013281175899)
XLA Ops:
  0.6 157.8 %shard_map.85 = (bf16[128,4096]{1,0:T(8,128)(2,1)S(1)}, f32[3,3,64,2048]{3,2,1,0:T(8,128)S(1)}, f32[3,3,64,2048]{3,2,1,0:T(8,128)S(1)}) custom-call(bf16[128,4096]{1,0:T(8,128)(2,1)} %bitcast.12, s32[1,128]{1,0:T(1,128)} %bitcast.13, f32[1,128]{1,0:T(1,128)} %bitcast.14, bf16[3,3,64,4096]{3,2,1,0:T(8,128)(2,1)} %bitcast.9, f32[3,3,64,2048]{3,2,1,0:T(8,128)} %bitcast.10, ...), custom_call_target="tpu_custom_call" | custom-call | tf_op jit(solution)/shard_map/pallas_call | solution.py:504
  158.5 4.0 %shard_map.86 = (bf16[128,4096]{1,0:T(8,128)(2,1)}, f32[3,3,64,2048]{3,2,1,0:T(8,128)}, f32[3,3,64,2048]{3,2,1,0:T(8,128)}) custom-call(bf16[128,4096]{1,0:T(8,128)(2,1)S(1)} %get-tuple-element.9.eov, f32[3,3,64,2048]{3,2,1,0:T(8,128)S(1)} %get-tuple-element.10.ob, f32[3,3,64,2048]{3,2,1,0:T(8,128)S(1)} %get-tuple-element.11.mb), custom_call_target="tpu_custom_call" | custom-call | tf_op jit(solution)/shard_map/pallas_call | solution.py:525
